TPU v7x, 32 devices: a whole 2x2x4 slice. The times are simulated.
32 devices in a mesh: seq: 16 (over z, y, x), tensor: 2 (over core).
Axes of the slice: x: 2, y: 2, z: 4, core: 2. Of those that a mesh axis runs over, the one named last changes fastest.
Arguments:
- hidden_in: bfloat16 [2048, 2560], P('seq', 'tensor'), may hold values from -6 to 6
- norm_gain: float32 [2560], replicated, may hold values from 0.1 to 1.9
- w_query: bfloat16 [2560, 2048], P(None, 'tensor'), may hold values from -0.125 to 0.125
- w_key: bfloat16 [2560, 1024], P(None, 'tensor'), may hold values from -0.125 to 0.125
- w_value: bfloat16 [2560, 1024], P(None, 'tensor'), may hold values from -0.125 to 0.125
- w_out: bfloat16 [2048, 2560], P('tensor'), may hold values from -0.125 to 0.125
- q_gain: float32 [128], replicated, may hold values from 0.1 to 1.9
- k_gain: float32 [128], replicated, may hold values from 0.1 to 1.9
- lengths: int32 [16], replicated, may hold values from 1 to 1536, 2048 in all
Outputs:
- attn_out: bfloat16 [2048, 2560], P(('seq', 'tensor'))
- key_cache: bfloat16 [2048, 1024], P('seq', 'tensor')
- value_cache: bfloat16 [2048, 1024], P('seq', 'tensor')
Inputs may be any that keep to these rules, and one draw needn't show every extreme that they name: The lengths sum to 2048 and the largest is exactly 1536.
All inputs are finite; a program needn't handle non-finite values.
Results may differ from a plain program's by a relative error of at most 0.015.
Values may be sent and summed in bfloat16 or wider, within the bound.
A program may use at most 64 MiB of HBM per device.

v0:
```python
import math

import jax
import jax.numpy as jnp
from jax import lax
from jax.sharding import PartitionSpec as P

rope_base = 1000000.0
norm_eps = 1e-06
masked = -1e30


def prompt_starts(lengths, token_pos):
    ends = jnp.cumsum(lengths)
    starts = ends - lengths
    before = (ends[None, :] <= token_pos[:, None]).astype(jnp.int32)
    segment = jnp.sum(before, axis=1)
    onehot = segment[:, None] == jnp.arange(lengths.shape[0], dtype=jnp.int32)[None, :]
    return jnp.sum(jnp.where(onehot, starts[None, :], 0), axis=1)


def head_norm_rope(values, gain, rel_pos):
    width = values.shape[-1]
    half = width // 2
    mean_sq = jnp.mean(values * values, axis=-1, keepdims=True)
    normed = values * lax.rsqrt(mean_sq + norm_eps) * gain
    freq = rope_base ** (-jnp.arange(half, dtype=jnp.float32) * 2.0 / width)
    angle = rel_pos.astype(jnp.float32)[:, None] * freq[None, :]
    cosine = jnp.cos(angle)[:, None, :]
    sine = jnp.sin(angle)[:, None, :]
    first = normed[..., :half]
    second = normed[..., half:]
    return jnp.concatenate(
        [first * cosine - second * sine, second * cosine + first * sine], axis=-1
    )


def on_device(hidden_in, norm_gain, w_query, w_key, w_value, w_out, q_gain, k_gain, lengths):
    tokens = hidden_in.shape[0]
    width = w_query.shape[0]
    head_dim = q_gain.shape[0]
    q_cols = w_query.shape[1]
    kv_cols = w_key.shape[1]
    kv_local = kv_cols // head_dim
    group = q_cols // kv_cols
    combined = jnp.concatenate([w_query, w_key, w_value], axis=1)
    piece = lax.all_gather(hidden_in, "tensor", axis=1, tiled=True)
    wide = piece.astype(jnp.float32)
    rows = combined
    scaled = (wide * norm_gain[None, :]).astype(jnp.bfloat16)
    acc = jnp.dot(scaled, rows, preferred_element_type=jnp.float32)
    acc, sumsq = (acc, jnp.sum(wide * wide, axis=1))
    proj = acc * lax.rsqrt(sumsq / width + norm_eps)[:, None]
    block_index = lax.axis_index("seq")
    token_pos = block_index * tokens + jnp.arange(tokens, dtype=jnp.int32)
    seg_start = prompt_starts(lengths, token_pos)
    rel_pos = token_pos - seg_start
    queries = head_norm_rope(
        proj[:, :q_cols].reshape(tokens, kv_local * group, head_dim), q_gain, rel_pos
    ).astype(jnp.bfloat16)
    keys = head_norm_rope(
        proj[:, q_cols : q_cols + kv_cols].reshape(tokens, kv_local, head_dim), k_gain, rel_pos
    ).astype(jnp.bfloat16)
    key_flat = keys.reshape(tokens, kv_cols)
    value_flat = proj[:, q_cols + kv_cols :].astype(jnp.bfloat16)
    query_grid = queries.reshape(tokens, kv_local, group, head_dim)
    inv_root = 1.0 / math.sqrt(head_dim)
    last_pos = jnp.max(token_pos)
    first_start = jnp.min(seg_start)

    def attend_block(carry, key_block, value_block, key_start):
        rows = key_block.shape[0]
        key_pos = key_start + jnp.arange(rows, dtype=jnp.int32)

        def compute(state):
            best, total, summed = state
            key_heads = key_block.reshape(rows, kv_local, head_dim)
            value_heads = value_block.reshape(rows, kv_local, head_dim)
            score = (
                jnp.einsum(
                    "qhgd,khd->hgqk", query_grid, key_heads, preferred_element_type=jnp.float32
                )
                * inv_root
            )
            visible = (key_pos[None, :] >= seg_start[:, None]) & (
                key_pos[None, :] <= token_pos[:, None]
            )
            score = jnp.where(visible[None, None], score, masked)
            fresh = jnp.maximum(best, jnp.max(score, axis=-1))
            weights = jnp.where(visible[None, None], jnp.exp(score - fresh[..., None]), 0.0)
            decay = jnp.exp(best - fresh)
            total = total * decay + jnp.sum(weights, axis=-1)
            summed = summed * decay[..., None] + jnp.einsum(
                "hgqk,khd->hgqd",
                weights.astype(jnp.bfloat16),
                value_heads,
                preferred_element_type=jnp.float32,
            )
            return (fresh, total, summed)

        seen = (key_start <= last_pos) & (key_start + rows - 1 >= first_start)
        return lax.cond(seen, compute, lambda state: state, carry)

    start_state = (
        jnp.full((kv_local, group, tokens), masked, jnp.float32),
        jnp.zeros((kv_local, group, tokens), jnp.float32),
        jnp.zeros((kv_local, group, tokens, head_dim), jnp.float32),
    )
    key_piece = lax.all_gather(key_flat, "seq", axis=0, tiled=True)
    value_piece = lax.all_gather(value_flat, "seq", axis=0, tiled=True)
    rows = key_piece.shape[0]
    size = math.gcd(rows, 512)
    count = rows // size

    def one_part(state, part):
        key_part, value_part, offset = part
        return (attend_block(state, key_part, value_part, offset), None)

    offsets = jnp.arange(count, dtype=jnp.int32) * size
    parts = (
        key_piece.reshape(count, size, kv_cols),
        value_piece.reshape(count, size, kv_cols),
        offsets,
    )
    state, unused = lax.scan(one_part, start_state, parts)
    best, total, summed = state
    attn = summed / total[..., None]
    attn = jnp.transpose(attn, (2, 0, 1, 3)).reshape(tokens, q_cols).astype(jnp.bfloat16)
    mixed = lax.psum_scatter(
        jnp.dot(attn, w_out, preferred_element_type=jnp.float32).astype(jnp.bfloat16),
        "tensor",
        scatter_dimension=0,
        tiled=True,
    )
    return (mixed, key_flat, value_flat)


def solution(mesh):
    placed = (
        P("seq", "tensor"),
        P(),
        P(None, "tensor"),
        P(None, "tensor"),
        P(None, "tensor"),
        P("tensor", None),
        P(),
        P(),
        P(),
    )
    return jax.shard_map(
        on_device,
        mesh=mesh,
        in_specs=placed,
        out_specs=(P(("seq", "tensor"), None), P("seq", "tensor"), P("seq", "tensor")),
        check_vma=False,
    )
```

profile of v0, /device:TPU:25, one launch (start us, length us, event | category | flops | bytes accessed | tf_op | source)
XLA Modules:
  0.0 195.4 jit_solution(2344054673404487221)
XLA Ops:
  7.2 0.7 copy.48
  9.6 2.8 %all_gather.9 = bf16[128,2560]{1,0:T(8,128)(2,1)S(1)} all-gather(bf16[128,1280]{1,0:T(8,128)(2,1)} %param.13), channel_id=1, replica_groups=mesh['seq'=16,'tensor'=2] {'tensor'}, dimensions={1}, use_global_device_ids=true | all-gather | bytes 983040 | tf_op jit(solution)/shard_map/all_gather | solution.py:47
  12.6 5.2 %fusion.19 = f32[128,2048]{1,0:T(8,128)S(1)} fusion(bf16[2560,512]{1,0:T(8,128)(2,1)} %param.17, bf16[2560,512]{1,0:T(8,128)(2,1)} %param.16, bf16[2560,1024]{1,0:T(8,128)(2,1)} %param.15, bf16[128,2560]{1,0:T(8,128)(2,1)S(1)} %all_gather.9, f32[2560]{0:T(1024)} %param.14, f32[128]{0:T(128)S(1)} %add_rsqrt_fusion.2), kind=kOutput, calls=%fused_computation.28 | convolution fusion | flops 1374879744 | bytes 12200448 | tf_op jit(solution)/shard_map/dot_general | solution.py:51
  19.2 0.7 copy.69
  20.7 0.7 fusion.27
  22.7 56.8 %all-gather.3.cloned.1.call-done = bf16[2048,512]{1,0:T(8,128)(2,1)} async-done(((bf16[128,512]{1,0:T(8,128)(2,1)}), bf16[2048,512]{1,0:T(8,128)(2,1)}) %all-gather.3.cloned.1.call-update) | async-done | bytes 2097168 | tf_op jit(solution)/shard_map/all_gather | solution.py:109
  79.5 2.8 %copy.55 = bf16[4,512,512]{1,2,0:T(8,128)(2,1)S(1)} copy(bf16[4,512,512]{2,1,0:T(8,128)(2,1)} %bitcast.54) | data formatting | bytes 4194304
  82.3 59.9 %all-gather.5.cloned.1.call-done = bf16[2048,512]{1,0:T(8,128)(2,1)} async-done(((bf16[128,512]{1,0:T(8,128)(2,1)}), bf16[2048,512]{1,0:T(8,128)(2,1)}) %all-gather.5.cloned.1.call-update) | async-done | bytes 2097168 | tf_op jit(solution)/shard_map/all_gather | solution.py:110
  142.3 4.1 %copy.56 = bf16[4,512,512]{1,2,0:T(8,128)(2,1)} copy(bf16[4,512,512]{2,1,0:T(8,128)(2,1)} %bitcast.55) | data formatting | bytes 4194304
  146.5 28.4 %while.19 = (s32[]{:T(128)}, f32[4,2,128]{2,1,0:T(2,128)S(1)}, f32[4,2,128]{2,1,0:T(2,128)S(1)}, f32[4,2,128,128]{3,2,1,0:T(8,128)S(1)}, s32[4]{0:T(128)S(1)}, /...) while((s32[]{:T(128)}, f32[4,2,128]{2,1,0:T(2,128)S(1)}, ...), condition=%wide.region_13.14_spmd.clone, body=%wide.region_8.13_spmd.clone.sunk | while | flops 275712640 | bytes 11086683 | solution.py:125
  149.6 3.9 %conditional.3 = ((f32[4,2,128]{2,1,0:T(2,128)S(1)}, f32[4,2,128]{2,1,0:T(2,128)S(1)}, f32[4,2,128,128]{3,2,1,0:T(8,128)S(1)})) conditional(s32[]{:T(128)} %convert_element_type.77, (f32[4,2,128]{2,1,0:T(2,128)S(1)}, f32[4,2,128]{2,1,0:T(2,128)S(1)}, f32[4,2,128,128]{3,2,1,0:T(8,128)S(1)}) %tuple.73, (s32[]{:T(128)}, s32[512]{0:T(512)S(1)}, ...), branch_computations={%region_9.9_spmd, %region_10.12_spmd} | conditional | flops 275712640 | bytes 11083820 | solution.py:102
  150.4 1.1 constant_dynamic-slice_fusion
  152.6 0.9 convolution_add_fusion
  156.7 3.9 %conditional.3 = ((f32[4,2,128]{2,1,0:T(2,128)S(1)}, f32[4,2,128]{2,1,0:T(2,128)S(1)}, f32[4,2,128,128]{3,2,1,0:T(8,128)S(1)})) conditional(s32[]{:T(128)} %convert_element_type.77, (f32[4,2,128]{2,1,0:T(2,128)S(1)}, f32[4,2,128]{2,1,0:T(2,128)S(1)}, f32[4,2,128,128]{3,2,1,0:T(8,128)S(1)}) %tuple.73, (s32[]{:T(128)}, s32[512]{0:T(512)S(1)}, ...), branch_computations={%region_9.9_spmd, %region_10.12_spmd} | conditional | flops 275712640 | bytes 11083820 | solution.py:102
  157.5 1.1 constant_dynamic-slice_fusion
  159.7 0.9 convolution_add_fusion
  163.8 3.9 %conditional.3 = ((f32[4,2,128]{2,1,0:T(2,128)S(1)}, f32[4,2,128]{2,1,0:T(2,128)S(1)}, f32[4,2,128,128]{3,2,1,0:T(8,128)S(1)})) conditional(s32[]{:T(128)} %convert_element_type.77, (f32[4,2,128]{2,1,0:T(2,128)S(1)}, f32[4,2,128]{2,1,0:T(2,128)S(1)}, f32[4,2,128,128]{3,2,1,0:T(8,128)S(1)}) %tuple.73, (s32[]{:T(128)}, s32[512]{0:T(512)S(1)}, ...), branch_computations={%region_9.9_spmd, %region_10.12_spmd} | conditional | flops 275712640 | bytes 11083820 | solution.py:102
  164.6 1.1 constant_dynamic-slice_fusion
  166.9 0.9 convolution_add_fusion
  170.9 3.9 %conditional.3 = ((f32[4,2,128]{2,1,0:T(2,128)S(1)}, f32[4,2,128]{2,1,0:T(2,128)S(1)}, f32[4,2,128,128]{3,2,1,0:T(8,128)S(1)})) conditional(s32[]{:T(128)} %convert_element_type.77, (f32[4,2,128]{2,1,0:T(2,128)S(1)}, f32[4,2,128]{2,1,0:T(2,128)S(1)}, f32[4,2,128,128]{3,2,1,0:T(8,128)S(1)}) %tuple.73, (s32[]{:T(128)}, s32[512]{0:T(512)S(1)}, ...), branch_computations={%region_9.9_spmd, %region_10.12_spmd} | conditional | flops 275712640 | bytes 11083820 | solution.py:102
  171.7 1.1 constant_dynamic-slice_fusion
  174.0 0.9 convolution_add_fusion
  175.2 4.2 %convolution_convert_fusion = bf16[128,2560]{1,0:T(8,128)(2,1)} fusion(bf16[128,1024]{0,1:T(8,128)(2,1)S(1)} %bitcast.57, bf16[1024,2560]{1,0:T(8,128)(2,1)} %param.18), kind=kOutput, calls=%fused_computation.27 | convolution fusion | flops 671416320 | bytes 6160384 | tf_op jit(solution)/shard_map/dot_general | solution.py:130
  179.4 9.5 %reduce-scatter.2.cloned.1.call-done = bf16[64,2560]{1,0:T(8,128)(2,1)} async-done(((bf16[128,2560]{1,0:T(8,128)(2,1)}), bf16[64,2560]{1,0:T(8,128)(2,1)}) %reduce-scatter.2.cloned.1.call-update) | async-done | bytes 327696 | tf_op jit(solution)/shard_map/reduce_scatter | solution.py:129
  (90 shorter events, 15.3 us)
Async XLA Ops:
  7.2 72.4 %all-gather.3.cloned.1.call-start = ((), (), s32[]{:S(2)}) async-start(), calls=%async_computation.1 | async-start | bytes 2228224 | tf_op jit(solution)/shard_map/all_gather | solution.py:109
  12.6 5.9 %copy-start.1 = (f32[128]{0:T(128)S(1)}, f32[128]{0:T(128)}, u32[]{:S(2)}) copy-start(f32[128]{0:T(128)} %param.20) | copy-start | bytes 1540
  19.0 3.0 %copy-start = (f32[128]{0:T(128)S(1)}, f32[128]{0:T(128)}, u32[]{:S(2)}) copy-start(f32[128]{0:T(128)} %param.19) | copy-start | bytes 1540
  19.9 122.4 %all-gather.5.cloned.1.call-start = ((), (), s32[]{:S(2)}) async-start(), calls=%async_computation.2 | async-start | bytes 2228224 | tf_op jit(solution)/shard_map/all_gather | solution.py:110
  20.6 168.3 %reduce-scatter.2.cloned.1.call-start = ((), (), s32[]{:S(2)}) async-start(), calls=%async_computation.3 | async-start | bytes 983040 | tf_op jit(solution)/shard_map/reduce_scatter | solution.py:129
Sparse Core Ops, SparseCore 0:
  20.0 59.4 all-gather.2
  82.9 59.3 all-gather.4
  179.5 9.3 reduce-scatter.1
where the time goes:
time: 195 us
  waiting for transfers between devices  126 us (65%)
  local copies, waits for them, and re-layouts  16.6 us (9%)
  matrix products  15.1 us (8%)
  between operations  14 us (7%)
  loops' own time  10.6 us (5%)
  other arithmetic  9.85 us (5%)
  blocking collectives  2.78 us (1%)
    all_gather x1, waiting for transfers between devices, on_device(): value_piece = lax.all_gather(value_flat, 'seq', axis=0, tiled=True)  59.9 us
    all_gather x1, waiting for transfers between devices, on_device(): key_piece = lax.all_gather(key_flat, 'seq', axis=0, tiled=True)  56.8 us
    another operation x1, loops' own time, on_device(): state, unused = lax.scan(one_part, start_state, parts)  10.3 us
    reduce_scatter x1, waiting for transfers between devices, on_device(): lax.psum_scatter(jnp.dot(attn, w_out, preferred_element_type=jnp.float32)...  9.54 us
    unnamed x9, local copies, waits for them, and re-layouts  7.75 us
    dynamic_slice x8, local copies, waits for them, and re-layouts, on_device(): state, unused = lax.scan(one_part, start_state, parts)  6.88 us
    dot_general x1, matrix products, on_device(): acc = jnp.dot(scaled, rows, preferred_element_type=jnp.float32)  5.16 us
    dot_general x1, matrix products, on_device(): jnp.dot(attn, w_out, preferred_element_type=jnp.float32)  4.21 us
  transfers between devices with their start and end apart: 3, of which 3 were waited for; matrix products, arithmetic and copies ran while one was open for 3% of the time, Pallas kernels for 0%

commit v1 on v0

--- a/solution.py
+++ b/solution.py
@@ -1,8 +1,12 @@
+import functools
 import math
 
 import jax
 import jax.numpy as jnp
+import numpy as np
 from jax import lax
+from jax.experimental import pallas as pl
+from jax.experimental.pallas import tpu as pltpu
 from jax.sharding import PartitionSpec as P
 
 rope_base = 1000000.0
@@ -135,7 +139,329 @@
     return (mixed, key_flat, value_flat)
 
 
+GROUP = 4
+
+
+def fused_kernel(
+    hid, gain, wq, wk, wv, wo, q_gain, k_gain, freq, lens,
+    out, key_out, value_out,
+    peer_hid, wq_v, wk_v, wv_v, wo_v, kv_send, q_send, kv_buf, q_buf, o_send, o_buf,
+    seg_q, acc, den, y_send, y_recv, y_mine,
+    w_sem, h_sem, kv_ssem, kv_rsem, q_ssem, q_rsem, z_ssem, z_rsem, o_ssem, o_rsem, y_ssem, y_rsem,
+):
+    f32, bf16 = jnp.float32, jnp.bfloat16
+    tok, feat = hid.shape
+    seq = lax.axis_index("seq")
+    core = lax.axis_index("tensor")
+    planes = kv_buf.shape[0] // GROUP
+    plane = seq // GROUP
+    place = seq % GROUP
+    mate = (seq, 1 - core)
+    above = (seq + GROUP, core)
+    below = (seq - GROUP, core)
+
+    def peer(d):
+        return (plane * GROUP + (place + d) % GROUP, core)
+
+    def copy(src, dst, ssem, rsem, device):
+        return pltpu.make_async_remote_copy(
+            src_ref=src, dst_ref=dst, send_sem=ssem, recv_sem=rsem,
+            device_id=device, device_id_type=pl.DeviceIdType.MESH,
+        )
+
+    halves = (core, 1 - core)
+    loads = {}
+    count = 0
+    for name, src, dst in (("k", wk, wk_v), ("v", wv, wv_v), ("q", wq, wq_v)):
+        for i in range(2):
+            loads[name, i] = pltpu.make_async_copy(
+                src.at[pl.ds(pl.multiple_of(halves[i] * feat, feat), feat)], dst.at[i], w_sem.at[count]
+            )
+            count += 1
+    for key in (("k", 0), ("v", 0), ("k", 1), ("v", 1), ("q", 0), ("q", 1)):
+        loads[key].start()
+    load_wo = pltpu.make_async_copy(wo, wo_v, w_sem.at[count])
+    load_wo.start()
+
+    barrier = pltpu.get_barrier_semaphore()
+
+    def greet(device):
+        pl.semaphore_signal(barrier, inc=1, device_id=device, device_id_type=pl.DeviceIdType.MESH)
+
+    greet(mate)
+    for d in range(1, GROUP):
+        greet(peer(d))
+
+    @pl.when(plane < planes - 1)
+    def _():
+        greet(above)
+
+    @pl.when(plane > 0)
+    def _():
+        greet(below)
+
+    neighbours = (plane + planes - 1) // planes + (2 * planes - 2 - plane) // planes
+    pl.semaphore_wait(barrier, GROUP + neighbours)
+
+    hid_copy = copy(hid, peer_hid, h_sem.at[0], h_sem.at[1], mate)
+    hid_copy.start()
+
+    lengths = [lens[j] for j in range(lens.shape[0])]
+    ends, run = [], jnp.int32(0)
+    for length in lengths:
+        run = run + length
+        ends.append(run)
+    for b in range(GROUP):
+        pos = lax.broadcasted_iota(jnp.int32, (tok, 128), 0) + (plane * GROUP + b) * tok
+        start = jnp.zeros((tok, 128), jnp.int32)
+        for length, end in zip(lengths, ends):
+            start = start + jnp.where(end <= pos, length, 0)
+        seg_q[b] = start
+    own_pos = lax.broadcasted_iota(jnp.int32, (tok, 128), 0) + seq * tok
+    angle = (own_pos - seg_q[place]).astype(f32) * freq[...]
+    cosine = jnp.cos(angle)
+    lane = lax.broadcasted_iota(jnp.int32, (tok, 128), 1)
+    sine = jnp.where(lane < 64, -jnp.sin(angle), jnp.sin(angle))
+
+    x_own = hid[...].astype(f32)
+    scaled_own = (x_own * gain[core]).astype(bf16)
+    sum_own = jnp.sum(x_own * x_own, axis=1, keepdims=True)
+    hid_copy.wait()
+    x_far = peer_hid[...].astype(f32)
+    scaled_far = (x_far * gain[1 - core]).astype(bf16)
+    sumsq = sum_own + jnp.sum(x_far * x_far, axis=1, keepdims=True)
+    inv = lax.rsqrt(sumsq / (2 * feat) + norm_eps)
+
+    def project(w, j):
+        cols = slice(j * 256, (j + 1) * 256)
+        total = jnp.dot(scaled_own, w[0, :, cols], preferred_element_type=f32)
+        total = total + jnp.dot(scaled_far, w[1, :, cols], preferred_element_type=f32)
+        return total * inv
+
+    def rope(u, g):
+        u = u * lax.rsqrt(jnp.mean(u * u, axis=1, keepdims=True) + norm_eps) * g[...]
+        return (u * cosine + pltpu.roll(u, 64, 1) * sine).astype(bf16)
+
+    for name in ("k", "v"):
+        for i in range(2):
+            loads[name, i].wait()
+    for j in range(2):
+        keys = project(wk_v, j)
+        values = project(wv_v, j).astype(bf16)
+        value_out[:, j * 256 : (j + 1) * 256] = values
+        for i in range(2):
+            head = 2 * j + i
+            key = rope(keys[:, i * 128 : (i + 1) * 128], k_gain)
+            key_out[:, head * 128 : (head + 1) * 128] = key
+            kv_send[head, :, :128] = key
+            kv_send[head, :, 128:] = values[:, i * 128 : (i + 1) * 128]
+
+    kv_buf[seq] = kv_send[place]
+
+    def up(k, d):
+        slot = kv_buf.at[(plane - k) * GROUP + (place + GROUP - d) % GROUP]
+        return copy(slot, slot, z_ssem.at[k, d], z_rsem.at[k, d], above)
+
+    def from_below(k, d):
+        slot = kv_buf.at[(plane - 1 - k) * GROUP + (place + GROUP - d) % GROUP]
+        return copy(slot, slot, z_ssem.at[k, d], z_rsem.at[k, d], below)
+
+    def send_up(k, d):
+        @pl.when(plane < planes - 1)
+        def _():
+            up(k, d).start()
+
+    kv_copies = {}
+    for d in range(1, GROUP):
+        kv_copies[d] = copy(
+            kv_send.at[(place + d) % GROUP], kv_buf.at[seq], kv_ssem.at[d], kv_rsem.at[d], peer(d)
+        )
+        kv_copies[d].start()
+    send_up(0, 0)
+
+    def kv_arrival(d):
+        slot = kv_buf.at[plane * GROUP + (place + GROUP - d) % GROUP]
+        return copy(slot, slot, kv_ssem.at[d], kv_rsem.at[d], peer(d))
+
+    for i in range(2):
+        loads["q", i].wait()
+    for j in range(GROUP):
+        pair = project(wq_v, j)
+        for i in range(2):
+            q_send[j, :, i * 128 : (i + 1) * 128] = rope(pair[:, i * 128 : (i + 1) * 128], q_gain)
+        if j >= 1:
+            kv_arrival(j).wait_recv()
+            send_up(0, j)
+    q_copies = {}
+    for d in range(1, GROUP):
+        q_copies[d] = copy(
+            q_send.at[(place + d) % GROUP], q_buf.at[place], q_ssem.at[d], q_rsem.at[d], peer(d)
+        )
+        q_copies[d].start()
+    q_buf[place] = q_send[place]
+    for d in range(1, GROUP):
+        slot = q_buf.at[(place + GROUP - d) % GROUP]
+        copy(slot, slot, q_ssem.at[d], q_rsem.at[d], peer(d)).wait_recv()
+
+    scale = math.log2(math.e) / math.sqrt(128)
+    span = GROUP * tok
+
+    def attend(k):
+        first = (plane - k) * GROUP
+        key_pos = lax.broadcasted_iota(jnp.int32, (tok, span), 1) + first * tok
+
+        def one_block(b, carry):
+            keys = kv_buf[pl.ds(first, GROUP), :, :128].reshape(span, 128)
+            values = kv_buf[pl.ds(first, GROUP), :, 128:].reshape(span, 128)
+            start = jnp.concatenate([seg_q[b]] * (span // 128), axis=1)
+            visible = key_pos >= start
+            if k == 0:
+                q_pos = lax.broadcasted_iota(jnp.int32, (tok, span), 0) + (first + b) * tok
+                visible = visible & (key_pos <= q_pos)
+            for h in range(2):
+                cols = slice(h * 128, (h + 1) * 128)
+                score = lax.dot_general(
+                    q_buf[b, :, cols], keys, (((1,), (1,)), ((), ())), preferred_element_type=f32
+                )
+                weights = jnp.where(visible, jnp.exp2(score * scale), 0.0)
+                part = weights[:, :128]
+                for i in range(1, span // 128):
+                    part = part + weights[:, i * 128 : (i + 1) * 128]
+                summed = jnp.dot(weights.astype(bf16), values, preferred_element_type=f32)
+                if k == 0:
+                    den[b, :, cols] = part
+                    acc[b, :, cols] = summed
+                else:
+                    den[b, :, cols] += part
+                    acc[b, :, cols] += summed
+            return carry
+
+        lax.fori_loop(0, GROUP, one_block, 0)
+
+    attend(0)
+    for k in range(1, planes):
+        @pl.when(k <= plane)
+        def _(k=k):
+            for d in range(GROUP):
+                from_below(k - 1, d).wait_recv()
+                if k < planes - 1:
+                    send_up(k, d)
+            attend(k)
+
+    def finish(b, dst):
+        for h in range(2):
+            cols = slice(h * 128, (h + 1) * 128)
+            total = jnp.sum(den[b, :, cols], axis=1, keepdims=True)
+            dst[b, :, cols] = (acc[b, :, cols] / total).astype(bf16)
+
+    o_copies = {}
+    for d in range(1, GROUP):
+        b = (place + d) % GROUP
+        finish(b, o_send)
+        o_copies[d] = copy(o_send.at[b], o_buf.at[place], o_ssem.at[d], o_rsem.at[d], peer(d))
+        o_copies[d].start()
+    finish(place, o_buf)
+    load_wo.wait()
+    for d in range(1, GROUP):
+        slot = o_buf.at[(place + GROUP - d) % GROUP]
+        copy(slot, slot, o_ssem.at[d], o_rsem.at[d], peer(d)).wait_recv()
+
+    part = y_send.shape[2]
+    half = tok // 2
+    y_copies = []
+    for n in range(y_send.shape[0]):
+        cols = slice(n * part, (n + 1) * part)
+        total = jnp.dot(o_buf[0], wo_v[0:256, cols], preferred_element_type=f32)
+        for b in range(1, GROUP):
+            total = total + jnp.dot(
+                o_buf[b], wo_v[b * 256 : (b + 1) * 256, cols], preferred_element_type=f32
+            )
+        y_send[n] = jnp.where(core == 0, total[half:], total[:half]).astype(bf16)
+        y_copies.append(copy(y_send.at[n], y_recv.at[n], y_ssem.at[n], y_rsem.at[n], mate))
+        y_copies[n].start()
+        y_mine[n] = jnp.where(core == 0, total[:half], total[half:])
+    for n in range(y_send.shape[0]):
+        y_copies[n].wait_recv()
+        out[:, n * part : (n + 1) * part] = (y_mine[n] + y_recv[n].astype(f32)).astype(bf16)
+    for n in range(y_send.shape[0]):
+        y_copies[n].wait_send()
+    for d in range(1, GROUP):
+        kv_copies[d].wait_send()
+        q_copies[d].wait_send()
+        o_copies[d].wait_send()
+    for k in range(planes - 1):
+        @pl.when((plane < planes - 1) & (k <= plane))
+        def _(k=k):
+            for d in range(GROUP):
+                up(k, d).wait_send()
+
+
+def on_device_fused(hidden_in, norm_gain, w_query, w_key, w_value, w_out, q_gain, k_gain, lengths, blocks=16):
+    tok, feat = hidden_in.shape
+    width = w_out.shape[1]
+    f32, bf16 = jnp.float32, jnp.bfloat16
+    half_freq = rope_base ** (-np.arange(64, dtype=np.float64) * 2.0 / 128)
+    freq = np.concatenate([half_freq, half_freq]).astype(np.float32)[None, :]
+    planes = blocks // GROUP
+    part = width // 5
+    vmem = pl.BlockSpec(memory_space=pltpu.VMEM)
+    any_space = pl.BlockSpec(memory_space=pl.ANY)
+    dma = pltpu.SemaphoreType.DMA
+    return pl.pallas_call(
+        fused_kernel,
+        out_shape=(
+            jax.ShapeDtypeStruct((tok // 2, width), bf16),
+            jax.ShapeDtypeStruct((tok, w_key.shape[1]), bf16),
+            jax.ShapeDtypeStruct((tok, w_value.shape[1]), bf16),
+        ),
+        in_specs=[vmem, vmem, any_space, any_space, any_space, any_space, vmem, vmem, vmem,
+                  pl.BlockSpec(memory_space=pltpu.SMEM)],
+        out_specs=(vmem, vmem, vmem),
+        scratch_shapes=[
+            pltpu.VMEM((tok, feat), bf16),
+            pltpu.VMEM((2, feat, w_query.shape[1]), bf16),
+            pltpu.VMEM((2, feat, w_key.shape[1]), bf16),
+            pltpu.VMEM((2, feat, w_value.shape[1]), bf16),
+            pltpu.VMEM(w_out.shape, bf16),
+            pltpu.VMEM((GROUP, tok, 256), bf16),
+            pltpu.VMEM((GROUP, tok, 256), bf16),
+            pltpu.VMEM((blocks, tok, 256), bf16),
+            pltpu.VMEM((GROUP, tok, 256), bf16),
+            pltpu.VMEM((GROUP, tok, 256), bf16),
+            pltpu.VMEM((GROUP, tok, 256), bf16),
+            pltpu.VMEM((GROUP, tok, 128), jnp.int32),
+            pltpu.VMEM((GROUP, tok, 256), f32),
+            pltpu.VMEM((GROUP, tok, 256), f32),
+            pltpu.VMEM((5, tok // 2, part), bf16),
+            pltpu.VMEM((5, tok // 2, part), bf16),
+            pltpu.VMEM((5, tok // 2, part), f32),
+            dma((7,)),
+            dma((2,)),
+            dma((GROUP,)),
+            dma((GROUP,)),
+            dma((GROUP,)),
+            dma((GROUP,)),
+            dma((planes - 1, GROUP)),
+            dma((planes - 1, GROUP)),
+            dma((GROUP,)),
+            dma((GROUP,)),
+            dma((5,)),
+            dma((5,)),
+        ],
+        compiler_params=pltpu.CompilerParams(
+            collective_id=0, has_side_effects=True, vmem_limit_bytes=44 * 1024 * 1024
+        ),
+        cost_estimate=pl.CostEstimate(
+            flops=3_100_000_000, bytes_accessed=17_000_000, transcendentals=2_200_000
+        ),
+    )(hidden_in, norm_gain.reshape(2, 1, feat), w_query, w_key, w_value, w_out,
+      q_gain.reshape(1, 128), k_gain.reshape(1, 128), freq, lengths)
+
+
 def solution(mesh):
+    seq, tensor = mesh.shape["seq"], mesh.shape["tensor"]
+    fits = tensor == 2 and seq % GROUP == 0 and seq <= 16
+    body = functools.partial(on_device_fused, blocks=seq) if fits else on_device
     placed = (
         P("seq", "tensor"),
         P(),
@@ -148,7 +474,7 @@
         P(),
     )
     return jax.shard_map(
-        on_device,
+        body,
         mesh=mesh,
         in_specs=placed,
         out_specs=(P(("seq", "tensor"), None), P("seq", "tensor"), P("seq", "tensor")),

time: 195 us -> 51 us (0.26)
  waiting for transfers between devices: 126 us -> 0 us
  Pallas kernels: 0 us -> 40.2 us
  matrix products: 15.1 us -> 0 us
  between operations: 14 us -> 0.65 us
  loops' own time: 10.6 us -> 0 us
  other arithmetic: 9.85 us -> 0 us
  local copies, waits for them, and re-layouts: 16.6 us -> 9.82 us
  blocking collectives: 2.78 us -> 0 us
    all_gather x2 -> x0, waiting for transfers between devices: 117 us -> none  [the longest x1 59.9 us: on_device(): value_piece = lax.all_gather(value_flat, 'seq', axis=0, tiled=True)]
    pallas_call x0 -> x1, Pallas kernels: none -> 40.2 us  [on_device_fused(): pl.pallas_call(fused_kernel, out_shape=(jax.ShapeDtypeStruct((tok // 2, w...]
    dot_general x10 -> x0, matrix products: 15.1 us -> none  [the longest x1 5.16 us: on_device(): acc = jnp.dot(scaled, rows, preferred_element_type=jnp.float32)]
    another operation x5 -> x0, loops' own time: 10.6 us -> none  [the longest x1 10.3 us: on_device(): state, unused = lax.scan(one_part, start_state, parts)]
    reduce_scatter x1 -> x0, waiting for transfers between devices: 9.54 us -> none  [on_device(): lax.psum_scatter(jnp.dot(attn, w_out, preferred_element_type=jnp.float32)...]
    dynamic_slice x8 -> x0, local copies, waits for them, and re-layouts: 6.88 us -> none  [on_device(): state, unused = lax.scan(one_part, start_state, parts)]
    reduce_sum x9 -> x0, other arithmetic: 2.88 us -> none  [the longest x4 2.08 us: compute(): total = total * decay + jnp.sum(weights, axis=-1)]
    all_gather x1 -> x0, blocking collectives: 2.78 us -> none  [on_device(): piece = lax.all_gather(hidden_in, 'tensor', axis=1, tiled=True)]
  transfers between devices with their start and end apart: 3 -> 0, of which waited for: 3 -> 0; matrix products, arithmetic and copies ran while one was open for 3% -> 0% of each run, Pallas kernels for 0% -> 0%
where the time goes in v1:
time: 51 us; the launch traced here: 50.7 us
  Pallas kernels  40.2 us (79%)
  local copies, waits for them, and re-layouts  9.82 us (19%)
  between operations  0.65 us (1%)
    pallas_call x1, Pallas kernels, on_device_fused(): pl.pallas_call(fused_kernel, out_shape=(jax.ShapeDtypeStruct((tok // 2, w...  40.2 us
    unnamed x17, local copies, waits for them, and re-layouts  9.1 us

profile of v1, /device:TPU:25, one launch (start us, length us, event | category | flops | bytes accessed | tf_op | source)
XLA Modules:
  0.0 50.7 jit_solution(16391140343956706121)
XLA Ops:
  0.6 0.7 %reshape.15.gain = f32[2,1,1280]{2,1,0:T(1,128)S(1)} reshape(f32[2560]{0:T(1024)} %param.11) | data formatting | bytes 20480 | tf_op jit(solution)/shard_map/reshape | solution.py:457
  1.4 0.0 copy-start
  1.4 1.7 %copy-done = bf16[2560,512]{1,0:T(8,128)(2,1)S(1)} copy-done((bf16[2560,512]{1,0:T(8,128)(2,1)S(1)}, bf16[2560,512]{1,0:T(8,128)(2,1)}, u32[]{:S(2)}) %copy-start) | copy-done | bytes 2621464
  3.1 0.0 copy-start.1
  3.1 1.7 %copy-done.1 = bf16[2560,512]{1,0:T(8,128)(2,1)S(1)} copy-done((bf16[2560,512]{1,0:T(8,128)(2,1)S(1)}, bf16[2560,512]{1,0:T(8,128)(2,1)}, u32[]{:S(2)}) %copy-start.1) | copy-done | bytes 2621464
  4.8 0.0 copy-start.2
  4.8 1.0 %copy-done.2 = bf16[128,1280]{1,0:T(8,128)(2,1)S(1)} copy-done((bf16[128,1280]{1,0:T(8,128)(2,1)S(1)}, bf16[128,1280]{1,0:T(8,128)(2,1)}, u32[]{:S(2)}) %copy-start.2) | copy-done | bytes 327704
  5.8 0.0 copy-start.3
  5.8 0.7 %copy-done.3 = f32[128]{0:T(128)S(1)} copy-done((f32[128]{0:T(128)S(1)}, f32[128]{0:T(128)}, u32[]{:S(2)}) %copy-start.3) | copy-done | bytes 536
  6.5 0.0 copy-start.4
  6.5 0.7 %copy-done.4 = f32[128]{0:T(128)S(1)} copy-done((f32[128]{0:T(128)S(1)}, f32[128]{0:T(128)}, u32[]{:S(2)}) %copy-start.4) | copy-done | bytes 536
  7.1 0.0 copy-start.5
  7.1 0.7 %copy-done.5 = s32[16]{0:T(128)S(1)} copy-done((s32[16]{0:T(128)S(1)}, s32[16]{0:T(128)}, u32[]{:S(2)}) %copy-start.5) | copy-done | bytes 88
  7.8 0.0 copy-start.6
  7.8 0.7 %copy-done.6 = f32[1,128]{1,0:T(1,128)S(1)} copy-done((f32[1,128]{1,0:T(1,128)S(1)}, f32[1,128]{1,0:T(1,128)}, u32[]{:S(2)}) %copy-start.6) | copy-done | bytes 536
  8.4 40.2 %shard_map.121 = (bf16[64,2560]{1,0:T(8,128)(2,1)S(1)}, bf16[128,512]{1,0:T(8,128)(2,1)S(1)}, bf16[128,512]{1,0:T(8,128)(2,1)S(1)}) custom-call(bf16[128,1280]{1,0:T(8,128)(2,1)S(1)} %copy-done.2, f32[2,1,1280]{2,1,0:T(1,128)S(1)} %reshape.15.gain, bf16[2560,1024]{1,0:T(8,128)(2,1)} %wq.1, bf16[2560,512]{1,0:T(8,128)(2,1)S(1)} %copy-done, ...), custom_call_target="tpu_custom_call" | custom-call | flops 3100000000 | bytes 17000000 | tf_op jit(solution)/shard_map/pallas_call | solution.py:410
  48.7 0.7 %copy.16 = bf16[64,2560]{1,0:T(8,128)(2,1)} copy(bf16[64,2560]{1,0:T(8,128)(2,1)S(1)} %get-tuple-element.6) | data formatting | bytes 655360
  49.4 0.7 %copy.17 = bf16[128,512]{1,0:T(8,128)(2,1)} copy(bf16[128,512]{1,0:T(8,128)(2,1)S(1)} %get-tuple-element.7) | data formatting | bytes 262144
  50.0 0.7 %copy.18 = bf16[128,512]{1,0:T(8,128)(2,1)} copy(bf16[128,512]{1,0:T(8,128)(2,1)S(1)} %get-tuple-element.8) | data formatting | bytes 262144
Async XLA Ops:
  1.4 1.7 %copy-start = (bf16[2560,512]{1,0:T(8,128)(2,1)S(1)}, bf16[2560,512]{1,0:T(8,128)(2,1)}, u32[]{:S(2)}) copy-start(bf16[2560,512]{1,0:T(8,128)(2,1)} %wk.1) | copy-start | bytes 7864324
  3.1 1.7 %copy-start.1 = (bf16[2560,512]{1,0:T(8,128)(2,1)S(1)}, bf16[2560,512]{1,0:T(8,128)(2,1)}, u32[]{:S(2)}) copy-start(bf16[2560,512]{1,0:T(8,128)(2,1)} %wv.1) | copy-start | bytes 7864324
  4.8 1.0 %copy-start.2 = (bf16[128,1280]{1,0:T(8,128)(2,1)S(1)}, bf16[128,1280]{1,0:T(8,128)(2,1)}, u32[]{:S(2)}) copy-start(bf16[128,1280]{1,0:T(8,128)(2,1)} %hid.1) | copy-start | bytes 983044
  5.8 0.7 %copy-start.3 = (f32[128]{0:T(128)S(1)}, f32[128]{0:T(128)}, u32[]{:S(2)}) copy-start(f32[128]{0:T(128)} %param.16) | copy-start | bytes 1540
  6.5 0.7 %copy-start.4 = (f32[128]{0:T(128)S(1)}, f32[128]{0:T(128)}, u32[]{:S(2)}) copy-start(f32[128]{0:T(128)} %param.17) | copy-start | bytes 1540
  7.1 0.7 %copy-start.5 = (s32[16]{0:T(128)S(1)}, s32[16]{0:T(128)}, u32[]{:S(2)}) copy-start(s32[16]{0:T(128)} %lens.1) | copy-start | bytes 196
  7.8 0.7 %copy-start.6 = (f32[1,128]{1,0:T(1,128)S(1)}, f32[1,128]{1,0:T(1,128)}, u32[]{:S(2)}) copy-start(f32[1,128]{1,0:T(1,128)} %constant.2.clone.freq) | copy-start | bytes 1540

commit v2 on v1

--- a/solution.py
+++ b/solution.py
@@ -143,11 +143,13 @@
 
 
 def fused_kernel(
-    hid, gain, wq, wk, wv, wo, q_gain, k_gain, freq, lens,
-    out, key_out, value_out,
-    peer_hid, wq_v, wk_v, wv_v, wo_v, kv_send, q_send, kv_buf, q_buf, o_send, o_buf,
-    seg_q, acc, den, y_send, y_recv, y_mine,
-    w_sem, h_sem, kv_ssem, kv_rsem, q_ssem, q_rsem, z_ssem, z_rsem, o_ssem, o_rsem, y_ssem, y_rsem,
+    hid_in, gain_in, wq, wk, wv, wo, q_gain_in, k_gain_in, freq_in, lens_in,
+    out_hbm, key_hbm, value_hbm,
+    out, key_out, value_out, hid, gain, q_gain, k_gain, freq, lens,
+    peer_hid, wq_v, wkv_v, wo_v, kv_send, q_send, kv_buf, q_buf, o_send, o_buf,
+    seg_q, acc, den, kv_acc, q_acc, y_send, y_recv, y_mine,
+    in_sem, wkv_sem, wq_sem, wo_sem, h_sem, kv_ssem, kv_rsem, q_ssem, q_rsem,
+    z_ssem, z_rsem, o_ssem, o_rsem, y_ssem, y_rsem, out_sem,
 ):
     f32, bf16 = jnp.float32, jnp.bfloat16
     tok, feat = hid.shape
@@ -169,20 +171,6 @@
             device_id=device, device_id_type=pl.DeviceIdType.MESH,
         )
 
-    halves = (core, 1 - core)
-    loads = {}
-    count = 0
-    for name, src, dst in (("k", wk, wk_v), ("v", wv, wv_v), ("q", wq, wq_v)):
-        for i in range(2):
-            loads[name, i] = pltpu.make_async_copy(
-                src.at[pl.ds(pl.multiple_of(halves[i] * feat, feat), feat)], dst.at[i], w_sem.at[count]
-            )
-            count += 1
-    for key in (("k", 0), ("v", 0), ("k", 1), ("v", 1), ("q", 0), ("q", 1)):
-        loads[key].start()
-    load_wo = pltpu.make_async_copy(wo, wo_v, w_sem.at[count])
-    load_wo.start()
-
     barrier = pltpu.get_barrier_semaphore()
 
     def greet(device):
@@ -200,11 +188,40 @@
     def _():
         greet(below)
 
-    neighbours = (plane + planes - 1) // planes + (2 * planes - 2 - plane) // planes
-    pl.semaphore_wait(barrier, GROUP + neighbours)
-
-    hid_copy = copy(hid, peer_hid, h_sem.at[0], h_sem.at[1], mate)
-    hid_copy.start()
+    halves = (core, 1 - core)
+    small = []
+    for src, dst in (
+        (hid_in, hid),
+        (lens_in, lens),
+        (freq_in, freq),
+        (gain_in.at[:, pl.ds(pl.multiple_of(halves[0] * feat, 128), feat)], gain.at[0]),
+        (gain_in.at[:, pl.ds(pl.multiple_of(halves[1] * feat, 128), feat)], gain.at[1]),
+        (q_gain_in, q_gain),
+        (k_gain_in, k_gain),
+    ):
+        small.append(pltpu.make_async_copy(src, dst, in_sem.at[len(small)]))
+        small[-1].start()
+
+    def rows(i):
+        return pl.ds(pl.multiple_of(halves[i] * feat, feat), feat)
+
+    kv_loads, q_loads = {}, {}
+    for i in range(2):
+        for d in range(GROUP):
+            cols = pl.ds(pl.multiple_of((place + d) % GROUP * 128, 128), 128)
+            for n, w in enumerate((wk, wv)):
+                kv_loads[i, d, n] = pltpu.make_async_copy(
+                    w.at[rows(i), cols], wkv_v.at[i, d, :, n * 128 : (n + 1) * 128], wkv_sem.at[i, d, n]
+                )
+                kv_loads[i, d, n].start()
+    for i in range(2):
+        q_loads[i] = pltpu.make_async_copy(wq.at[rows(i)], wq_v.at[i], wq_sem.at[i])
+        q_loads[i].start()
+    load_wo = pltpu.make_async_copy(wo, wo_v, wo_sem)
+    load_wo.start()
+
+    for load in small:
+        load.wait()
 
     lengths = [lens[j] for j in range(lens.shape[0])]
     ends, run = [], jnp.int32(0)
@@ -224,39 +241,34 @@
     sine = jnp.where(lane < 64, -jnp.sin(angle), jnp.sin(angle))
 
     x_own = hid[...].astype(f32)
-    scaled_own = (x_own * gain[core]).astype(bf16)
+    scaled_own = (x_own * gain[0]).astype(bf16)
     sum_own = jnp.sum(x_own * x_own, axis=1, keepdims=True)
+    for d in range(GROUP):
+        for n in range(2):
+            kv_loads[0, d, n].wait()
+        kv_acc[d] = jnp.dot(scaled_own, wkv_v[0, d], preferred_element_type=f32)
+
+    neighbours = (plane + planes - 1) // planes + (2 * planes - 2 - plane) // planes
+    pl.semaphore_wait(barrier, GROUP + neighbours)
+    hid_copy = copy(hid, peer_hid, h_sem.at[0], h_sem.at[1], mate)
+    hid_copy.start()
+
+    def q_cols(d):
+        return pl.ds(pl.multiple_of((place + d) % GROUP * 256, 256), 256)
+
+    q_loads[0].wait()
+    for d in range(GROUP):
+        q_acc[d] = jnp.dot(scaled_own, wq_v[0, :, q_cols(d)], preferred_element_type=f32)
+
     hid_copy.wait()
     x_far = peer_hid[...].astype(f32)
-    scaled_far = (x_far * gain[1 - core]).astype(bf16)
+    scaled_far = (x_far * gain[1]).astype(bf16)
     sumsq = sum_own + jnp.sum(x_far * x_far, axis=1, keepdims=True)
     inv = lax.rsqrt(sumsq / (2 * feat) + norm_eps)
-
-    def project(w, j):
-        cols = slice(j * 256, (j + 1) * 256)
-        total = jnp.dot(scaled_own, w[0, :, cols], preferred_element_type=f32)
-        total = total + jnp.dot(scaled_far, w[1, :, cols], preferred_element_type=f32)
-        return total * inv
 
     def rope(u, g):
         u = u * lax.rsqrt(jnp.mean(u * u, axis=1, keepdims=True) + norm_eps) * g[...]
         return (u * cosine + pltpu.roll(u, 64, 1) * sine).astype(bf16)
-
-    for name in ("k", "v"):
-        for i in range(2):
-            loads[name, i].wait()
-    for j in range(2):
-        keys = project(wk_v, j)
-        values = project(wv_v, j).astype(bf16)
-        value_out[:, j * 256 : (j + 1) * 256] = values
-        for i in range(2):
-            head = 2 * j + i
-            key = rope(keys[:, i * 128 : (i + 1) * 128], k_gain)
-            key_out[:, head * 128 : (head + 1) * 128] = key
-            kv_send[head, :, :128] = key
-            kv_send[head, :, 128:] = values[:, i * 128 : (i + 1) * 128]
-
-    kv_buf[seq] = kv_send[place]
 
     def up(k, d):
         slot = kv_buf.at[(plane - k) * GROUP + (place + GROUP - d) % GROUP]
@@ -271,100 +283,144 @@
         def _():
             up(k, d).start()
 
-    kv_copies = {}
-    for d in range(1, GROUP):
-        kv_copies[d] = copy(
-            kv_send.at[(place + d) % GROUP], kv_buf.at[seq], kv_ssem.at[d], kv_rsem.at[d], peer(d)
-        )
-        kv_copies[d].start()
-    send_up(0, 0)
+    kv_copies, q_copies = {}, {}
+    for d in range(GROUP):
+        for n in range(2):
+            kv_loads[1, d, n].wait()
+        pair = kv_acc[d] + jnp.dot(scaled_far, wkv_v[1, d], preferred_element_type=f32)
+        pair = pair * inv
+        key = rope(pair[:, :128], k_gain)
+        value = pair[:, 128:].astype(bf16)
+        cols = pl.ds(pl.multiple_of((place + d) % GROUP * 128, 128), 128)
+        key_out[:, cols] = key
+        value_out[:, cols] = value
+        if d == 0:
+            kv_buf[seq, :, :128] = key
+            kv_buf[seq, :, 128:] = value
+            send_up(0, 0)
+        else:
+            kv_send[d, :, :128] = key
+            kv_send[d, :, 128:] = value
+            kv_copies[d] = copy(kv_send.at[d], kv_buf.at[seq], kv_ssem.at[d], kv_rsem.at[d], peer(d))
+            kv_copies[d].start()
+
+    stores = [
+        pltpu.make_async_copy(src, dst, out_sem.at[n])
+        for n, (src, dst) in enumerate(((key_out, key_hbm), (value_out, value_hbm), (out, out_hbm)))
+    ]
+    stores[0].start()
+    stores[1].start()
 
     def kv_arrival(d):
         slot = kv_buf.at[plane * GROUP + (place + GROUP - d) % GROUP]
         return copy(slot, slot, kv_ssem.at[d], kv_rsem.at[d], peer(d))
 
-    for i in range(2):
-        loads["q", i].wait()
-    for j in range(GROUP):
-        pair = project(wq_v, j)
+    q_loads[1].wait()
+    for turn, d in enumerate((1, 2, 3, 0)):
+        pair = q_acc[d] + jnp.dot(scaled_far, wq_v[1, :, q_cols(d)], preferred_element_type=f32)
+        pair = pair * inv
         for i in range(2):
-            q_send[j, :, i * 128 : (i + 1) * 128] = rope(pair[:, i * 128 : (i + 1) * 128], q_gain)
-        if j >= 1:
-            kv_arrival(j).wait_recv()
-            send_up(0, j)
-    q_copies = {}
-    for d in range(1, GROUP):
-        q_copies[d] = copy(
-            q_send.at[(place + d) % GROUP], q_buf.at[place], q_ssem.at[d], q_rsem.at[d], peer(d)
-        )
-        q_copies[d].start()
-    q_buf[place] = q_send[place]
+            query = rope(pair[:, i * 128 : (i + 1) * 128], q_gain)
+            if d == 0:
+                q_buf[place, i * tok : (i + 1) * tok] = query
+            else:
+                q_send[d, i * tok : (i + 1) * tok] = query
+        if d > 0:
+            q_copies[d] = copy(q_send.at[d], q_buf.at[place], q_ssem.at[d], q_rsem.at[d], peer(d))
+            q_copies[d].start()
+        if turn >= 1:
+            kv_arrival(turn).wait_recv()
+            send_up(0, turn)
+
+    @pl.when(plane >= 1)
+    def _():
+        for d in range(GROUP):
+            from_below(0, d).wait_recv()
+            send_up(1, d)
+
     for d in range(1, GROUP):
         slot = q_buf.at[(place + GROUP - d) % GROUP]
         copy(slot, slot, q_ssem.at[d], q_rsem.at[d], peer(d)).wait_recv()
 
     scale = math.log2(math.e) / math.sqrt(128)
-    span = GROUP * tok
-
-    def attend(k):
-        first = (plane - k) * GROUP
-        key_pos = lax.broadcasted_iota(jnp.int32, (tok, span), 1) + first * tok
-
-        def one_block(b, carry):
-            keys = kv_buf[pl.ds(first, GROUP), :, :128].reshape(span, 128)
-            values = kv_buf[pl.ds(first, GROUP), :, 128:].reshape(span, 128)
-            start = jnp.concatenate([seg_q[b]] * (span // 128), axis=1)
+
+    def o_copy(i):
+        b = (place + 1 + i) % GROUP
+        return copy(o_send.at[b], o_buf.at[place], o_ssem.at[i], o_rsem.at[i], (plane * GROUP + b, core))
+
+    def attend(k, pieces, ends_plane):
+        slots = [(plane - k) * GROUP + (place + GROUP - d) % GROUP for d in pieces]
+        span = 128 * len(pieces)
+        lanes = lax.broadcasted_iota(jnp.int32, (tok, 128), 1)
+        key_pos = jnp.concatenate([lanes + slot * tok for slot in slots], axis=1)
+        fresh = k == 0 and pieces[0] == 0
+
+        def one_block(i, carry):
+            b = (place + 1 + i) % GROUP
+            keys = jnp.concatenate([kv_buf[slot, :, :128] for slot in slots], axis=0)
+            values = jnp.concatenate([kv_buf[slot, :, 128:] for slot in slots], axis=0)
+            start = jnp.concatenate([seg_q[b]] * len(pieces), axis=1)
             visible = key_pos >= start
             if k == 0:
-                q_pos = lax.broadcasted_iota(jnp.int32, (tok, span), 0) + (first + b) * tok
+                q_pos = lax.broadcasted_iota(jnp.int32, (tok, span), 0) + (plane * GROUP + b) * tok
                 visible = visible & (key_pos <= q_pos)
+            score = lax.dot_general(
+                q_buf[b], keys, (((1,), (1,)), ((), ())), preferred_element_type=f32
+            )
+            rounded = []
             for h in range(2):
-                cols = slice(h * 128, (h + 1) * 128)
-                score = lax.dot_general(
-                    q_buf[b, :, cols], keys, (((1,), (1,)), ((), ())), preferred_element_type=f32
-                )
-                weights = jnp.where(visible, jnp.exp2(score * scale), 0.0)
+                weights = jnp.where(visible, jnp.exp2(score[h * tok : (h + 1) * tok] * scale), 0.0)
                 part = weights[:, :128]
-                for i in range(1, span // 128):
-                    part = part + weights[:, i * 128 : (i + 1) * 128]
-                summed = jnp.dot(weights.astype(bf16), values, preferred_element_type=f32)
-                if k == 0:
-                    den[b, :, cols] = part
-                    acc[b, :, cols] = summed
+                for n in range(1, len(pieces)):
+                    part = part + weights[:, n * 128 : (n + 1) * 128]
+                if fresh:
+                    den[b, h * tok : (h + 1) * tok] = part
                 else:
-                    den[b, :, cols] += part
-                    acc[b, :, cols] += summed
+                    den[b, h * tok : (h + 1) * tok] += part
+                rounded.append(weights.astype(bf16))
+            summed = jnp.dot(jnp.concatenate(rounded, axis=0), values, preferred_element_type=f32)
+            if fresh:
+                acc[b] = summed
+            else:
+                acc[b] += summed
+            if ends_plane:
+                @pl.when(plane == k)
+                def _():
+                    for h in range(2):
+                        part = slice(h * tok, (h + 1) * tok)
+                        total = jnp.sum(den[b, part], axis=1, keepdims=True)
+                        o_send[b, :, h * 128 : (h + 1) * 128] = (acc[b, part] / total).astype(bf16)
+
+                    @pl.when(i < GROUP - 1)
+                    def _():
+                        o_copy(i).start()
+
             return carry
 
         lax.fori_loop(0, GROUP, one_block, 0)
 
-    attend(0)
+    attend(0, (0, 1, 2, 3), True)
     for k in range(1, planes):
         @pl.when(k <= plane)
         def _(k=k):
-            for d in range(GROUP):
-                from_below(k - 1, d).wait_recv()
-                if k < planes - 1:
-                    send_up(k, d)
-            attend(k)
-
-    def finish(b, dst):
-        for h in range(2):
-            cols = slice(h * 128, (h + 1) * 128)
-            total = jnp.sum(den[b, :, cols], axis=1, keepdims=True)
-            dst[b, :, cols] = (acc[b, :, cols] / total).astype(bf16)
-
-    o_copies = {}
-    for d in range(1, GROUP):
-        b = (place + d) % GROUP
-        finish(b, o_send)
-        o_copies[d] = copy(o_send.at[b], o_buf.at[place], o_ssem.at[d], o_rsem.at[d], peer(d))
-        o_copies[d].start()
-    finish(place, o_buf)
+            if k < planes - 1:
+                if k > 1:
+                    for d in range(GROUP):
+                        from_below(k - 1, d).wait_recv()
+                        send_up(k, d)
+                attend(k, (0, 1, 2, 3), True)
+            else:
+                for pieces in ((0, 1, 2), (3,)):
+                    for d in pieces:
+                        if k > 1:
+                            from_below(k - 1, d).wait_recv()
+                    attend(k, pieces, pieces[-1] == GROUP - 1)
+
+    o_buf[place] = o_send[place]
     load_wo.wait()
-    for d in range(1, GROUP):
-        slot = o_buf.at[(place + GROUP - d) % GROUP]
-        copy(slot, slot, o_ssem.at[d], o_rsem.at[d], peer(d)).wait_recv()
+    for i in range(GROUP - 1):
+        slot = o_buf.at[(place + 2 * GROUP - 1 - i) % GROUP]
+        copy(slot, slot, o_ssem.at[i], o_rsem.at[i], peer(i + 1)).wait_recv()
 
     part = y_send.shape[2]
     half = tok // 2
@@ -383,17 +439,31 @@
     for n in range(y_send.shape[0]):
         y_copies[n].wait_recv()
         out[:, n * part : (n + 1) * part] = (y_mine[n] + y_recv[n].astype(f32)).astype(bf16)
+    stores[2].start()
     for n in range(y_send.shape[0]):
         y_copies[n].wait_send()
     for d in range(1, GROUP):
         kv_copies[d].wait_send()
         q_copies[d].wait_send()
-        o_copies[d].wait_send()
+        o_copy(d - 1).wait_send()
     for k in range(planes - 1):
         @pl.when((plane < planes - 1) & (k <= plane))
         def _(k=k):
             for d in range(GROUP):
                 up(k, d).wait_send()
+    for store in stores:
+        store.wait()
+
+
+def store_kernel(a, b, c, a_out, b_out, c_out, sem):
+    stores = [
+        pltpu.make_async_copy(src, dst, sem.at[n])
+        for n, (src, dst) in enumerate(((a, a_out), (b, b_out), (c, c_out)))
+    ]
+    for store in stores:
+        store.start()
+    for store in stores:
+        store.wait()
 
 
 def on_device_fused(hidden_in, norm_gain, w_query, w_key, w_value, w_out, q_gain, k_gain, lengths, blocks=16):
@@ -404,38 +474,48 @@
     freq = np.concatenate([half_freq, half_freq]).astype(np.float32)[None, :]
     planes = blocks // GROUP
     part = width // 5
-    vmem = pl.BlockSpec(memory_space=pltpu.VMEM)
-    any_space = pl.BlockSpec(memory_space=pl.ANY)
+    hbm = pl.BlockSpec(memory_space=pltpu.HBM)
     dma = pltpu.SemaphoreType.DMA
-    return pl.pallas_call(
+    shapes = (
+        jax.ShapeDtypeStruct((tok // 2, width), bf16),
+        jax.ShapeDtypeStruct((tok, w_key.shape[1]), bf16),
+        jax.ShapeDtypeStruct((tok, w_value.shape[1]), bf16),
+    )
+    results = pl.pallas_call(
         fused_kernel,
-        out_shape=(
-            jax.ShapeDtypeStruct((tok // 2, width), bf16),
-            jax.ShapeDtypeStruct((tok, w_key.shape[1]), bf16),
-            jax.ShapeDtypeStruct((tok, w_value.shape[1]), bf16),
-        ),
-        in_specs=[vmem, vmem, any_space, any_space, any_space, any_space, vmem, vmem, vmem,
-                  pl.BlockSpec(memory_space=pltpu.SMEM)],
-        out_specs=(vmem, vmem, vmem),
+        out_shape=shapes,
+        in_specs=[hbm] * 10,
+        out_specs=(hbm, hbm, hbm),
         scratch_shapes=[
+            *[pltpu.VMEM(shape.shape, bf16) for shape in shapes],
+            pltpu.VMEM((tok, feat), bf16),
+            pltpu.VMEM((2, 1, feat), f32),
+            pltpu.VMEM((1, 128), f32),
+            pltpu.VMEM((1, 128), f32),
+            pltpu.VMEM((1, 128), f32),
+            pltpu.SMEM(lengths.shape, jnp.int32),
             pltpu.VMEM((tok, feat), bf16),
             pltpu.VMEM((2, feat, w_query.shape[1]), bf16),
-            pltpu.VMEM((2, feat, w_key.shape[1]), bf16),
-            pltpu.VMEM((2, feat, w_value.shape[1]), bf16),
+            pltpu.VMEM((2, GROUP, feat, 256), bf16),
             pltpu.VMEM(w_out.shape, bf16),
             pltpu.VMEM((GROUP, tok, 256), bf16),
-            pltpu.VMEM((GROUP, tok, 256), bf16),
+            pltpu.VMEM((GROUP, 2 * tok, 128), bf16),
             pltpu.VMEM((blocks, tok, 256), bf16),
-            pltpu.VMEM((GROUP, tok, 256), bf16),
+            pltpu.VMEM((GROUP, 2 * tok, 128), bf16),
             pltpu.VMEM((GROUP, tok, 256), bf16),
             pltpu.VMEM((GROUP, tok, 256), bf16),
             pltpu.VMEM((GROUP, tok, 128), jnp.int32),
+            pltpu.VMEM((GROUP, 2 * tok, 128), f32),
+            pltpu.VMEM((GROUP, 2 * tok, 128), f32),
             pltpu.VMEM((GROUP, tok, 256), f32),
             pltpu.VMEM((GROUP, tok, 256), f32),
             pltpu.VMEM((5, tok // 2, part), bf16),
             pltpu.VMEM((5, tok // 2, part), bf16),
             pltpu.VMEM((5, tok // 2, part), f32),
             dma((7,)),
+            dma((2, GROUP, 2)),
+            dma((2,)),
+            dma,
             dma((2,)),
             dma((GROUP,)),
             dma((GROUP,)),
@@ -447,15 +527,24 @@
             dma((GROUP,)),
             dma((5,)),
             dma((5,)),
+            dma((3,)),
         ],
         compiler_params=pltpu.CompilerParams(
-            collective_id=0, has_side_effects=True, vmem_limit_bytes=44 * 1024 * 1024
+            collective_id=0, has_side_effects=True, vmem_limit_bytes=63 * 1024 * 1024
         ),
         cost_estimate=pl.CostEstimate(
             flops=3_100_000_000, bytes_accessed=17_000_000, transcendentals=2_200_000
         ),
-    )(hidden_in, norm_gain.reshape(2, 1, feat), w_query, w_key, w_value, w_out,
+    )(hidden_in, norm_gain.reshape(1, 2 * feat), w_query, w_key, w_value, w_out,
       q_gain.reshape(1, 128), k_gain.reshape(1, 128), freq, lengths)
+    return pl.pallas_call(
+        store_kernel,
+        out_shape=shapes,
+        in_specs=[pl.BlockSpec(memory_space=pl.ANY)] * 3,
+        out_specs=(hbm, hbm, hbm),
+        scratch_shapes=[dma((3,))],
+        compiler_params=pltpu.CompilerParams(vmem_limit_bytes=63 * 1024 * 1024),
+    )(*results)
 
 
 def solution(mesh):

time: 51 us -> 60.1 us (1.18)
  Pallas kernels: 40.2 us -> 57.9 us
  local copies, waits for them, and re-layouts: 9.82 us -> 1.31 us
    pallas_call x1 -> x2, Pallas kernels: 40.2 us -> 57.9 us  [the longest x1 38.9 us: on_device_fused(): pl.pallas_call(fused_kernel, out_shape=shapes, in_specs=[hbm] * 10, out_s...]
    unnamed x17 -> x0, local copies, waits for them, and re-layouts: 9.1 us -> none
where the time goes in v2:
time: 60.1 us; the launch traced here: 59.8 us
  Pallas kernels  57.9 us (96%)
  local copies, waits for them, and re-layouts  1.31 us (2%)
  between operations  0.64 us (1%)
    pallas_call x1, Pallas kernels, on_device_fused(): pl.pallas_call(fused_kernel, out_shape=shapes, in_specs=[hbm] * 10, out_s...  38.9 us
    pallas_call x1, Pallas kernels, on_device_fused(): pl.pallas_call(store_kernel, out_shape=shapes, in_specs=[pl.BlockSpec(mem...  19 us
    reshape x1, local copies, waits for them, and re-layouts, on_device_fused(): norm_gain.reshape(1, 2 * feat)  1.31 us

profile of v2, /device:TPU:25, one launch (start us, length us, event | category | flops | bytes accessed | tf_op | source)
XLA Modules:
  0.0 59.8 jit_solution(8675963704080721812)
XLA Ops:
  0.6 1.3 %reshape.15.gain_in = f32[1,2560]{1,0:T(1,128)} reshape(f32[2560]{0:T(1024)} %param.11) | data formatting | bytes 20480 | tf_op jit(solution)/shard_map/reshape | solution.py:538
  1.9 38.9 %shard_map.121 = (bf16[64,2560]{1,0:T(8,128)(2,1)}, bf16[128,512]{1,0:T(8,128)(2,1)}, bf16[128,512]{1,0:T(8,128)(2,1)}) custom-call(bf16[128,1280]{1,0:T(8,128)(2,1)} %hid_in.1, f32[1,2560]{1,0:T(1,128)} %reshape.15.gain_in, bf16[2560,1024]{1,0:T(8,128)(2,1)} %wq.1, bf16[2560,512]{1,0:T(8,128)(2,1)} %wk.1, bf16[2560,512]{1,0:T(8,128)(2,1)} %wv.1, ...), custom_call_target="tpu_custom_call" | custom-call | flops 3100000000 | bytes 17000000 | tf_op jit(solution)/shard_map/pallas_call | solution.py:484
  40.8 19.0 %shard_map.122 = (bf16[64,2560]{1,0:T(8,128)(2,1)}, bf16[128,512]{1,0:T(8,128)(2,1)}, bf16[128,512]{1,0:T(8,128)(2,1)}) custom-call(bf16[64,2560]{1,0:T(8,128)(2,1)} %get-tuple-element.6.a, bf16[128,512]{1,0:T(8,128)(2,1)} %get-tuple-element.7.b, bf16[128,512]{1,0:T(8,128)(2,1)} %get-tuple-element.8.c), custom_call_target="tpu_custom_call" | custom-call | tf_op jit(solution)/shard_map/pallas_call | solution.py:540

commit v3 on v2

--- a/solution.py
+++ b/solution.py
@@ -147,7 +147,7 @@
     out_hbm, key_hbm, value_hbm,
     out, key_out, value_out, hid, gain, q_gain, k_gain, freq, lens,
     peer_hid, wq_v, wkv_v, wo_v, kv_send, q_send, kv_buf, q_buf, o_send, o_buf,
-    seg_q, acc, den, kv_acc, q_acc, y_send, y_recv, y_mine,
+    seg_q, acc, den, kv_acc, y_acc, y_send, y_recv, y_mine,
     in_sem, wkv_sem, wq_sem, wo_sem, h_sem, kv_ssem, kv_rsem, q_ssem, q_rsem,
     z_ssem, z_rsem, o_ssem, o_rsem, y_ssem, y_rsem, out_sem,
 ):
@@ -194,8 +194,7 @@
         (hid_in, hid),
         (lens_in, lens),
         (freq_in, freq),
-        (gain_in.at[:, pl.ds(pl.multiple_of(halves[0] * feat, 128), feat)], gain.at[0]),
-        (gain_in.at[:, pl.ds(pl.multiple_of(halves[1] * feat, 128), feat)], gain.at[1]),
+        (gain_in, gain),
         (q_gain_in, q_gain),
         (k_gain_in, k_gain),
     ):
@@ -240,29 +239,29 @@
     lane = lax.broadcasted_iota(jnp.int32, (tok, 128), 1)
     sine = jnp.where(lane < 64, -jnp.sin(angle), jnp.sin(angle))
 
+    neighbours = (plane + planes - 1) // planes + (2 * planes - 2 - plane) // planes
+    pl.semaphore_wait(barrier, GROUP + neighbours)
+    hid_copy = copy(hid, peer_hid, h_sem.at[0], h_sem.at[1], mate)
+    hid_copy.start()
+
+    def gain_row(half):
+        first = half * (feat // 128)
+        return jnp.concatenate([gain[pl.ds(first + r, 1)] for r in range(feat // 128)], axis=1)
+
     x_own = hid[...].astype(f32)
-    scaled_own = (x_own * gain[0]).astype(bf16)
+    scaled_own = (x_own * gain_row(halves[0])).astype(bf16)
     sum_own = jnp.sum(x_own * x_own, axis=1, keepdims=True)
     for d in range(GROUP):
         for n in range(2):
             kv_loads[0, d, n].wait()
         kv_acc[d] = jnp.dot(scaled_own, wkv_v[0, d], preferred_element_type=f32)
 
-    neighbours = (plane + planes - 1) // planes + (2 * planes - 2 - plane) // planes
-    pl.semaphore_wait(barrier, GROUP + neighbours)
-    hid_copy = copy(hid, peer_hid, h_sem.at[0], h_sem.at[1], mate)
-    hid_copy.start()
-
     def q_cols(d):
         return pl.ds(pl.multiple_of((place + d) % GROUP * 256, 256), 256)
 
-    q_loads[0].wait()
-    for d in range(GROUP):
-        q_acc[d] = jnp.dot(scaled_own, wq_v[0, :, q_cols(d)], preferred_element_type=f32)
-
     hid_copy.wait()
     x_far = peer_hid[...].astype(f32)
-    scaled_far = (x_far * gain[1]).astype(bf16)
+    scaled_far = (x_far * gain_row(halves[1])).astype(bf16)
     sumsq = sum_own + jnp.sum(x_far * x_far, axis=1, keepdims=True)
     inv = lax.rsqrt(sumsq / (2 * feat) + norm_eps)
 
@@ -315,9 +314,11 @@
         slot = kv_buf.at[plane * GROUP + (place + GROUP - d) % GROUP]
         return copy(slot, slot, kv_ssem.at[d], kv_rsem.at[d], peer(d))
 
+    q_loads[0].wait()
     q_loads[1].wait()
     for turn, d in enumerate((1, 2, 3, 0)):
-        pair = q_acc[d] + jnp.dot(scaled_far, wq_v[1, :, q_cols(d)], preferred_element_type=f32)
+        pair = jnp.dot(scaled_own, wq_v[0, :, q_cols(d)], preferred_element_type=f32)
+        pair = pair + jnp.dot(scaled_far, wq_v[1, :, q_cols(d)], preferred_element_type=f32)
         pair = pair * inv
         for i in range(2):
             query = rope(pair[:, i * 128 : (i + 1) * 128], q_gain)
@@ -416,22 +417,28 @@
                             from_below(k - 1, d).wait_recv()
                     attend(k, pieces, pieces[-1] == GROUP - 1)
 
-    o_buf[place] = o_send[place]
     load_wo.wait()
-    for i in range(GROUP - 1):
-        slot = o_buf.at[(place + 2 * GROUP - 1 - i) % GROUP]
-        copy(slot, slot, o_ssem.at[i], o_rsem.at[i], peer(i + 1)).wait_recv()
-
     part = y_send.shape[2]
     half = tok // 2
+
+    def head_group(heads, group, n):
+        rows = pl.ds(pl.multiple_of(group * 256, 256), 256)
+        return jnp.dot(heads, wo_v[rows, n * part : (n + 1) * part], preferred_element_type=f32)
+
+    for n in range(y_send.shape[0]):
+        y_acc[n] = head_group(o_send[place], place, n)
+    for i in range(GROUP - 2):
+        group = (place + 2 * GROUP - 1 - i) % GROUP
+        slot = o_buf.at[group]
+        copy(slot, slot, o_ssem.at[i], o_rsem.at[i], peer(i + 1)).wait_recv()
+        for n in range(y_send.shape[0]):
+            y_acc[n] += head_group(o_buf[group], group, n)
+    group = (place + 1) % GROUP
+    slot = o_buf.at[group]
+    copy(slot, slot, o_ssem.at[GROUP - 2], o_rsem.at[GROUP - 2], peer(GROUP - 1)).wait_recv()
     y_copies = []
     for n in range(y_send.shape[0]):
-        cols = slice(n * part, (n + 1) * part)
-        total = jnp.dot(o_buf[0], wo_v[0:256, cols], preferred_element_type=f32)
-        for b in range(1, GROUP):
-            total = total + jnp.dot(
-                o_buf[b], wo_v[b * 256 : (b + 1) * 256, cols], preferred_element_type=f32
-            )
+        total = y_acc[n] + head_group(o_buf[group], group, n)
         y_send[n] = jnp.where(core == 0, total[half:], total[:half]).astype(bf16)
         y_copies.append(copy(y_send.at[n], y_recv.at[n], y_ssem.at[n], y_rsem.at[n], mate))
         y_copies[n].start()
@@ -455,12 +462,14 @@
         store.wait()
 
 
-def store_kernel(a, b, c, a_out, b_out, c_out, sem):
-    stores = [
-        pltpu.make_async_copy(src, dst, sem.at[n])
-        for n, (src, dst) in enumerate(((a, a_out), (b, b_out), (c, c_out)))
-    ]
-    for store in stores:
+def store_kernel(a, b, c, a_out, b_out, c_out, a_held, b_held, c_held, in_sem, out_sem):
+    parts = ((a, a_held, a_out), (b, b_held, b_out), (c, c_held, c_out))
+    loads = [pltpu.make_async_copy(src, held, in_sem.at[n]) for n, (src, held, _) in enumerate(parts)]
+    stores = [pltpu.make_async_copy(held, dst, out_sem.at[n]) for n, (_, held, dst) in enumerate(parts)]
+    for load in loads:
+        load.start()
+    for load, store in zip(loads, stores):
+        load.wait()
         store.start()
     for store in stores:
         store.wait()
@@ -489,7 +498,7 @@
         scratch_shapes=[
             *[pltpu.VMEM(shape.shape, bf16) for shape in shapes],
             pltpu.VMEM((tok, feat), bf16),
-            pltpu.VMEM((2, 1, feat), f32),
+            pltpu.VMEM((2 * feat // 128, 128), f32),
             pltpu.VMEM((1, 128), f32),
             pltpu.VMEM((1, 128), f32),
             pltpu.VMEM((1, 128), f32),
@@ -508,11 +517,11 @@
             pltpu.VMEM((GROUP, 2 * tok, 128), f32),
             pltpu.VMEM((GROUP, 2 * tok, 128), f32),
             pltpu.VMEM((GROUP, tok, 256), f32),
-            pltpu.VMEM((GROUP, tok, 256), f32),
+            pltpu.VMEM((5, tok, part), f32),
             pltpu.VMEM((5, tok // 2, part), bf16),
             pltpu.VMEM((5, tok // 2, part), bf16),
             pltpu.VMEM((5, tok // 2, part), f32),
-            dma((7,)),
+            dma((6,)),
             dma((2, GROUP, 2)),
             dma((2,)),
             dma,
@@ -535,14 +544,14 @@
         cost_estimate=pl.CostEstimate(
             flops=3_100_000_000, bytes_accessed=17_000_000, transcendentals=2_200_000
         ),
-    )(hidden_in, norm_gain.reshape(1, 2 * feat), w_query, w_key, w_value, w_out,
+    )(hidden_in, norm_gain.reshape(2 * feat // 128, 128), w_query, w_key, w_value, w_out,
       q_gain.reshape(1, 128), k_gain.reshape(1, 128), freq, lengths)
     return pl.pallas_call(
         store_kernel,
         out_shape=shapes,
         in_specs=[pl.BlockSpec(memory_space=pl.ANY)] * 3,
         out_specs=(hbm, hbm, hbm),
-        scratch_shapes=[dma((3,))],
+        scratch_shapes=[*[pltpu.VMEM(shape.shape, bf16) for shape in shapes], dma((3,)), dma((3,))],
         compiler_params=pltpu.CompilerParams(vmem_limit_bytes=63 * 1024 * 1024),
     )(*results)
 

time: 60.1 us -> 39.9 us (0.66)
  Pallas kernels: 57.9 us -> 39.1 us
  local copies, waits for them, and re-layouts: 1.31 us -> 0 us
    pallas_call x1, Pallas kernels: 19 us -> 1.83 us  [on_device_fused(): pl.pallas_call(store_kernel, out_shape=shapes, in_specs=[pl.BlockSpec(mem...]
    pallas_call x1, Pallas kernels: 38.9 us -> 37.3 us  [on_device_fused(): pl.pallas_call(fused_kernel, out_shape=shapes, in_specs=[hbm] * 10, out_s...]
    reshape x1 -> x0, local copies, waits for them, and re-layouts: 1.31 us -> none  [on_device_fused(): norm_gain.reshape(1, 2 * feat)]
where the time goes in v3:
time: 39.9 us; the launch traced here: 39.7 us
  Pallas kernels  39.1 us (98%)
  between operations  0.64 us (2%)
    pallas_call x1, Pallas kernels, on_device_fused(): pl.pallas_call(fused_kernel, out_shape=shapes, in_specs=[hbm] * 10, out_s...  37.3 us
    pallas_call x1, Pallas kernels, on_device_fused(): pl.pallas_call(store_kernel, out_shape=shapes, in_specs=[pl.BlockSpec(mem...  1.83 us

profile of v3, /device:TPU:25, one launch (start us, length us, event | category | flops | bytes accessed | tf_op | source)
XLA Modules:
  0.0 39.7 jit_solution(634121494709421873)
XLA Ops:
  0.6 37.3 %shard_map.121 = (bf16[64,2560]{1,0:T(8,128)(2,1)}, bf16[128,512]{1,0:T(8,128)(2,1)}, bf16[128,512]{1,0:T(8,128)(2,1)}) custom-call(bf16[128,1280]{1,0:T(8,128)(2,1)} %hid_in.1, f32[20,128]{1,0:T(8,128)} %bitcast.3, bf16[2560,1024]{1,0:T(8,128)(2,1)} %wq.1, bf16[2560,512]{1,0:T(8,128)(2,1)} %wk.1, bf16[2560,512]{1,0:T(8,128)(2,1)} %wv.1, ...), custom_call_target="tpu_custom_call" | custom-call | flops 3100000000 | bytes 17000000 | tf_op jit(solution)/shard_map/pallas_call | solution.py:493
  37.9 1.8 %shard_map.122 = (bf16[64,2560]{1,0:T(8,128)(2,1)}, bf16[128,512]{1,0:T(8,128)(2,1)}, bf16[128,512]{1,0:T(8,128)(2,1)}) custom-call(bf16[64,2560]{1,0:T(8,128)(2,1)} %get-tuple-element.6.a, bf16[128,512]{1,0:T(8,128)(2,1)} %get-tuple-element.7.b, bf16[128,512]{1,0:T(8,128)(2,1)} %get-tuple-element.8.c), custom_call_target="tpu_custom_call" | custom-call | tf_op jit(solution)/shard_map/pallas_call | solution.py:549

commit v4 on v3

--- a/solution.py
+++ b/solution.py
@@ -233,11 +233,6 @@
         for length, end in zip(lengths, ends):
             start = start + jnp.where(end <= pos, length, 0)
         seg_q[b] = start
-    own_pos = lax.broadcasted_iota(jnp.int32, (tok, 128), 0) + seq * tok
-    angle = (own_pos - seg_q[place]).astype(f32) * freq[...]
-    cosine = jnp.cos(angle)
-    lane = lax.broadcasted_iota(jnp.int32, (tok, 128), 1)
-    sine = jnp.where(lane < 64, -jnp.sin(angle), jnp.sin(angle))
 
     neighbours = (plane + planes - 1) // planes + (2 * planes - 2 - plane) // planes
     pl.semaphore_wait(barrier, GROUP + neighbours)
@@ -254,6 +249,13 @@
     for d in range(GROUP):
         for n in range(2):
             kv_loads[0, d, n].wait()
+    own_pos = lax.broadcasted_iota(jnp.int32, (tok, 128), 0) + seq * tok
+    angle = (own_pos - seg_q[place]).astype(f32) * freq[...]
+    cosine = jnp.cos(angle)
+    sine = jnp.sin(angle)
+    lane = lax.broadcasted_iota(jnp.int32, (tok, 128), 1)
+    sine = jnp.where(lane < 64, -sine, sine)
+    for d in range(GROUP):
         kv_acc[d] = jnp.dot(scaled_own, wkv_v[0, d], preferred_element_type=f32)
 
     def q_cols(d):
@@ -329,13 +331,19 @@
         if d > 0:
             q_copies[d] = copy(q_send.at[d], q_buf.at[place], q_ssem.at[d], q_rsem.at[d], peer(d))
             q_copies[d].start()
-        if turn >= 1:
-            kv_arrival(turn).wait_recv()
-            send_up(0, turn)
+        if turn == 0:
+            @pl.when(plane >= 1)
+            def _():
+                from_below(0, 0).wait_recv()
+                send_up(1, 0)
+
+        if turn < GROUP - 1:
+            kv_arrival(turn + 1).wait_recv()
+            send_up(0, turn + 1)
 
     @pl.when(plane >= 1)
     def _():
-        for d in range(GROUP):
+        for d in range(1, GROUP):
             from_below(0, d).wait_recv()
             send_up(1, d)
 

time: 39.9 us -> 38.3 us (0.960)
  Pallas kernels: 39.1 us -> 37.5 us
    pallas_call x1, Pallas kernels: 37.3 us -> 35.7 us  [on_device_fused(): pl.pallas_call(fused_kernel, out_shape=shapes, in_specs=[hbm] * 10, out_s...]
where the time goes in v4:
time: 38.3 us; the launch traced here: 38.2 us
  Pallas kernels  37.5 us (98%)
  between operations  0.64 us (2%)
    pallas_call x1, Pallas kernels, on_device_fused(): pl.pallas_call(fused_kernel, out_shape=shapes, in_specs=[hbm] * 10, out_s...  35.7 us
    pallas_call x1, Pallas kernels, on_device_fused(): pl.pallas_call(store_kernel, out_shape=shapes, in_specs=[pl.BlockSpec(mem...  1.83 us

profile of v4, /device:TPU:25, one launch (start us, length us, event | category | flops | bytes accessed | tf_op | source)
XLA Modules:
  0.0 38.2 jit_solution(4834174606925020065)
XLA Ops:
  0.6 35.7 %shard_map.121 = (bf16[64,2560]{1,0:T(8,128)(2,1)}, bf16[128,512]{1,0:T(8,128)(2,1)}, bf16[128,512]{1,0:T(8,128)(2,1)}) custom-call(bf16[128,1280]{1,0:T(8,128)(2,1)} %hid_in.1, f32[20,128]{1,0:T(8,128)} %bitcast.3, bf16[2560,1024]{1,0:T(8,128)(2,1)} %wq.1, bf16[2560,512]{1,0:T(8,128)(2,1)} %wk.1, bf16[2560,512]{1,0:T(8,128)(2,1)} %wv.1, ...), custom_call_target="tpu_custom_call" | custom-call | flops 3100000000 | bytes 17000000 | tf_op jit(solution)/shard_map/pallas_call | solution.py:501
  36.4 1.8 %shard_map.122 = (bf16[64,2560]{1,0:T(8,128)(2,1)}, bf16[128,512]{1,0:T(8,128)(2,1)}, bf16[128,512]{1,0:T(8,128)(2,1)}) custom-call(bf16[64,2560]{1,0:T(8,128)(2,1)} %get-tuple-element.6.a, bf16[128,512]{1,0:T(8,128)(2,1)} %get-tuple-element.7.b, bf16[128,512]{1,0:T(8,128)(2,1)} %get-tuple-element.8.c), custom_call_target="tpu_custom_call" | custom-call | tf_op jit(solution)/shard_map/pallas_call | solution.py:557
